TPU v7x, 32 devices: a whole 2x2x4 slice. The times are simulated.
32 devices in a mesh: wave: 32 (over z, y, x, core), lev: 1.
Axes of the slice: x: 2, y: 2, z: 4, core: 2. Of those that a mesh axis runs over, the one named last changes fastest.
Arguments:
- spectra: bfloat16 [640, 16, 2, 640], P('wave', 'lev'), may hold values from -0.3125 to 0.3125
- legendre: bfloat16 [640, 32, 640], P('wave'), may hold values from -0.25 to 0.25
- wave_slots: int32 [640], replicated, may hold values from 0 to 639, each once
- row_cycle: int32 [32], replicated, may hold values from 0 to 1279, as said below
Outputs:
- grid_fields: bfloat16 [16, 32, 6144], P(None, 'wave', 'lev')
Inputs may be any that keep to these rules, and one draw needn't show every extreme that they name: `wave_slots`: each wavenumber 0 to 639 stands in exactly one slot; slot r lies on wave index r // 20. `row_cycle`: cycle numbers of distinct rows differ; cycle 0 and cycle 1280 - 1 both occur; row q lies on wave index q.
All inputs are finite; a program needn't handle non-finite values.
Results may differ from a plain program's by a relative error of at most 0.0055.
Values may be sent and summed in bfloat16 or wider, within the bound.
A program may use at most 64 MiB of HBM per device.

v0:
```python
from functools import partial
import math
import jax
import jax.numpy as jnp
from jax import lax
from jax.sharding import PartitionSpec as P

NLON = 6144
two_pi = 2.0 * math.pi


def twiddle_table(slot_waves, row_points, first_col, col_count):
    columns = first_col + lax.iota(jnp.int32, col_count)
    phase_int = slot_waves[:, None] * columns[None, :] % row_points
    angles = jnp.float32(two_pi) * phase_int.astype(jnp.float32) / row_points.astype(jnp.float32)
    weight = jnp.where(slot_waves == 0, jnp.float32(1.0), jnp.float32(2.0))[:, None]
    inside = (columns < row_points)[None, :]
    cosine = jnp.where(inside, weight * jnp.cos(angles), jnp.float32(0.0))
    sine_part = jnp.where(inside, -weight * jnp.sin(angles), jnp.float32(0.0))
    return jnp.concatenate([cosine, sine_part], axis=0).astype(jnp.bfloat16)


def row_product(coeffs, twiddle):
    return jnp.dot(coeffs, twiddle, preferred_element_type=jnp.float32).astype(jnp.bfloat16)


def shards(spectra, legendre, wave_slots, row_cycle):
    slots_dev, pairs_dev, two_parts, degrees = spectra.shape
    wave_count = lax.axis_size("wave")
    level_count = lax.axis_size("lev")
    total_slots = slots_dev * wave_count
    wave_pos = lax.axis_index("wave")
    level_pos = lax.axis_index("lev")
    own_waves = lax.dynamic_slice_in_dim(wave_slots, wave_pos * slots_dev, slots_dev)
    degree = lax.iota(jnp.int32, degrees)
    keep_mask = degree[None, :] < (total_slots - own_waves)[:, None]
    masked = jnp.where(keep_mask[:, None, None, :], spectra, jnp.zeros((), spectra.dtype))
    fourier = jnp.einsum(
        "rpik,rlk->plir", masked, legendre, preferred_element_type=jnp.float32
    ).astype(jnp.bfloat16)
    by_rows = lax.all_to_all(fourier, "wave", split_axis=1, concat_axis=3, tiled=True)
    rows_dev = by_rows.shape[1]
    flat_width = 2 * total_slots
    own_cycles = lax.dynamic_slice_in_dim(row_cycle, wave_pos * rows_dev, rows_dev)
    region = NLON // level_count
    first_col = level_pos * region
    actives = []
    row_pos = 0
    row_points = 20 + 4 * own_cycles[row_pos]
    active = first_col < row_points
    twiddle = twiddle_table(wave_slots, row_points, first_col, region)
    tables = [twiddle]
    actives.append(active)
    piece = lax.all_gather(by_rows, "lev", axis=0, tiled=True)
    row_pos = 0
    coeffs = piece[:, row_pos].reshape(piece.shape[0], flat_width)
    product = partial(row_product, coeffs, tables[row_pos])
    results = [product()]
    return jnp.stack(results, axis=1)


def solution(mesh):
    placed = (P("wave", "lev", None, None), P("wave", None, None), P(), P())
    return jax.shard_map(
        shards, mesh=mesh, in_specs=placed, out_specs=P(None, "wave", "lev"), check_vma=False
    )
```

profile of v0, /device:TPU:0, one launch (start us, length us, event | category | flops | bytes accessed | tf_op | source)
XLA Modules:
  0.0 236.1 jit_solution(6809609361605725039)
XLA Ops:
  0.0 0.0 copy-start
  0.0 0.8 dynamic-slice_subtract_fusion
  0.8 0.1 iota_compare_fusion
  0.9 1.9 broadcast_select_fusion
  2.8 0.0 copy-done
  2.8 0.4 fusion.17
  3.2 0.6 copy.12
  3.7 1.0 reshape.32
  4.7 7.3 %all-to-all-start = ((bf16[32,2,320]{2,1,0:T(2,128)(2,1)}), bf16[32,2,320]{2,1,0:T(2,128)(2,1)S(1)}, u32[]{:S(2)}, u32[]{:S(2)}) async-start(bf16[32,2,320]{2,1,0:T(2,128)(2,1)} %reshape.32), calls=%async_computation | async-start | bytes 98304 | tf_op jit(solution)/shard_map/all_to_all | solution.py:41
  12.0 1.3 dynamic_slice.7
  13.9 0.7 compare_select_fusion
  14.6 213.3 %select_convert_fusion.1 = (bf16[640,6144]{1,0:T(8,128)(2,1)}, bf16[640,6144]{1,0:T(8,128)(2,1)}) fusion(f32[640]{0:T(1024)S(1)} %get-tuple-element.7, f32[]{:T(128)S(6)} %convert_element_type.19, pred[]{:T(512)S(6)} %lt.49, s32[]{:T(128)S(6)} %select_n.34, s32[640]{0:T(1024)} %param.6, pred[6144]{0:T(1024)(128)(4,1)S(1)} %iota_compare_fusion.1, ...), kind=kLoop, calls=%fused_computation.9 | loop fusion | flops 66846720 | bytes 15742473 | tf_op jit(solution)/shard_map/convert
  227.9 0.0 all-to-all-done
  227.9 0.4 reshape.33
  228.3 0.1 copy.13
  228.4 0.3 reshape_squeeze.3
  228.8 7.4 %fusion.14 = bf16[16,1,6144]{2,0,1:T(8,128)(2,1)} fusion(bf16[16,1280]{1,0:T(8,128)(2,1)S(1)} %reshape_squeeze.3, bf16[640,6144]{1,0:T(8,128)(2,1)} %get-tuple-element.6, bf16[640,6144]{1,0:T(8,128)(2,1)} %get-tuple-element.5), kind=kOutput, calls=%fused_computation.16 | convolution fusion | flops 283213824 | bytes 15966208 | tf_op jit(solution)/shard_map/dot_general | solution.py:24
  (2 shorter events, 0.0 us)
Async XLA Ops:
  0.0 2.8 %copy-start = (bf16[20,32,640]{2,1,0:T(8,128)(2,1)S(1)}, bf16[20,32,640]{2,1,0:T(8,128)(2,1)}, u32[]{:S(2)}) copy-start(bf16[20,32,640]{2,1,0:T(8,128)(2,1)} %param.5) | copy-start | bytes 2457604
  4.7 223.2 %all-to-all-start = ((bf16[32,2,320]{2,1,0:T(2,128)(2,1)}), bf16[32,2,320]{2,1,0:T(2,128)(2,1)S(1)}, u32[]{:S(2)}, u32[]{:S(2)}) async-start(bf16[32,2,320]{2,1,0:T(2,128)(2,1)} %reshape.32), calls=%async_computation | async-start | bytes 98304 | tf_op jit(solution)/shard_map/all_to_all | solution.py:41
where the time goes:
time: 236 us
  other arithmetic  217 us (92%)
  matrix products  7.76 us (3%)
  starting transfers between devices  7.3 us (3%)
  local copies, waits for them, and re-layouts  3.6 us (2%)
    another operation x1, other arithmetic  213 us
    dot_general x1, matrix products, row_product(): jnp.dot(coeffs, twiddle, preferred_element_type=jnp.float32)  7.38 us
    all_to_all x1, starting transfers between devices, shards(): lax.all_to_all(fourier, 'wave', split_axis=1, concat_axis=3, tiled=True)  7.3 us
  transfers between devices with their start and end apart: 1, of which 0 were waited for; matrix products, arithmetic and copies ran while one was open for 91% of the time, Pallas kernels for 0%

commit v1 on v0

--- a/solution.py
+++ b/solution.py
@@ -1,3 +1,4 @@
+import functools
 from functools import partial
 import math
 import jax
@@ -7,6 +8,18 @@
 
 NLON = 6144
 two_pi = 2.0 * math.pi
+
+
+def watch_sheet(unit, dev_axis):
+    left_arr = lax.axis_size(dev_axis)
+    kept_arr = jnp.split(unit, left_arr, 1)
+    u1 = jnp.stack(kept_arr, 0)
+    f_next = lax.all_to_all(u1, concat_axis=0, axis_name=dev_axis, split_axis=0)
+    a_next = jnp.concatenate(f_next, 3)
+    return a_next
+
+
+direct_the_lots_all = functools.partial(watch_sheet, dev_axis="wave")
 
 
 def twiddle_table(slot_waves, row_points, first_col, col_count):
@@ -38,7 +51,7 @@
     fourier = jnp.einsum(
         "rpik,rlk->plir", masked, legendre, preferred_element_type=jnp.float32
     ).astype(jnp.bfloat16)
-    by_rows = lax.all_to_all(fourier, "wave", split_axis=1, concat_axis=3, tiled=True)
+    by_rows = direct_the_lots_all(fourier)
     rows_dev = by_rows.shape[1]
     flat_width = 2 * total_slots
     own_cycles = lax.dynamic_slice_in_dim(row_cycle, wave_pos * rows_dev, rows_dev)

time: 236 us -> 297 us (1.26)
  local copies, waits for them, and re-layouts: 3.6 us -> 65 us
    split x0 -> x33, local copies, waits for them, and re-layouts: none -> 28.7 us  [watch_sheet(): kept_arr = jnp.split(unit, left_arr, 1)]
    unnamed x4 -> x37, local copies, waits for them, and re-layouts: 1.32 us -> 24.3 us
    another operation x0 -> x33, local copies, waits for them, and re-layouts: none -> 10.3 us  [watch_sheet(): u1 = jnp.stack(kept_arr, 0)]
  transfers between devices with their start and end apart: 1 -> 1, of which waited for: 0 -> 0; matrix products, arithmetic and copies ran while one was open for 91% -> 72% of each run, Pallas kernels for 0% -> 0%
where the time goes in v1:
time: 297 us; the launch traced here: 296 us
  other arithmetic  215 us (72%)
  local copies, waits for them, and re-layouts  65 us (22%)
  matrix products  7.76 us (3%)
  starting transfers between devices  7.3 us (2%)
    another operation x1, other arithmetic  213 us
    split x33, local copies, waits for them, and re-layouts, watch_sheet(): kept_arr = jnp.split(unit, left_arr, 1)  28.7 us
    unnamed x37, local copies, waits for them, and re-layouts  24.3 us
    another operation x33, local copies, waits for them, and re-layouts, watch_sheet(): u1 = jnp.stack(kept_arr, 0)  10.3 us
    dot_general x1, matrix products, row_product(): jnp.dot(coeffs, twiddle, preferred_element_type=jnp.float32)  7.38 us
    all_to_all x1, starting transfers between devices, watch_sheet(): f_next = lax.all_to_all(u1, concat_axis=0, axis_name=dev_axis, split_axis=0)  7.3 us
  transfers between devices with their start and end apart: 1, of which 0 were waited for; matrix products, arithmetic and copies ran while one was open for 72% of the time, Pallas kernels for 0%

profile of v1, /device:TPU:0, one launch (start us, length us, event | category | flops | bytes accessed | tf_op | source)
XLA Modules:
  0.0 296.1 jit_solution(18302508579050607357)
XLA Ops:
  0.0 0.8 dynamic-slice_subtract_fusion
  0.9 1.9 broadcast_select_fusion
  3.2 1.8 fusion.23
  5.0 1.7 fusion.22
  6.7 1.2 copy.1568
  8.0 1.2 copy.1567
  9.4 1.2 copy.1566
  10.7 1.2 copy.1565
  12.1 1.2 copy.1564
  13.4 1.2 copy.1563
  14.8 1.2 copy.1562
  16.0 0.7 copy.1593
  16.7 1.2 copy.1561
  17.9 0.7 copy.1592
  18.6 1.2 copy.1560
  19.9 0.7 copy.1591
  20.6 1.2 copy.1559
  21.8 0.7 copy.1590
  22.5 1.2 copy.1558
  23.7 0.7 copy.1589
  24.4 1.2 copy.1557
  25.7 0.7 copy.1588
  27.0 1.2 copy.1587
  28.3 1.2 copy.1586
  29.6 1.8 copy.1585
  31.5 0.8 copy.1616
  32.3 0.9 copy.1584
  33.2 0.8 copy.1615
  40.8 1.3 constant_dynamic-update-slice_fusion.30
  42.1 1.3 constant_dynamic-update-slice_fusion.29
  43.4 1.3 constant_dynamic-update-slice_fusion.28
  44.7 1.3 constant_dynamic-update-slice_fusion.27
  46.0 1.3 constant_dynamic-update-slice_fusion.26
  47.3 1.3 constant_dynamic-update-slice_fusion.25
  49.2 0.6 constant_dynamic-update-slice_fusion.23
  50.4 0.6 constant_dynamic-update-slice_fusion.21
  54.7 0.6 constant_dynamic-update-slice_fusion.14
  55.9 0.6 constant_dynamic-update-slice_fusion.12
  58.9 0.6 constant_dynamic-update-slice_fusion.7
  59.5 0.6 constant_dynamic-update-slice_fusion.6
  60.1 0.6 constant_dynamic-update-slice_fusion.5
  60.7 0.6 constant_dynamic-update-slice_fusion.4
  63.7 1.4 copy.1619
  65.2 1.0 reshape.38
  66.1 7.3 %all-to-all-start = ((bf16[32,2,320]{2,1,0:T(2,128)(2,1)}), bf16[32,2,320]{2,1,0:T(2,128)(2,1)S(1)}, u32[]{:S(2)}, u32[]{:S(2)}) async-start(bf16[32,2,320]{2,1,0:T(2,128)(2,1)} %reshape.38), calls=%async_computation | async-start | bytes 98304 | tf_op jit(solution)/shard_map/all_to_all | solution.py:17
  73.4 1.2 dynamic_slice.7
  75.3 212.6 %select_convert_fusion.1 = (bf16[640,6144]{1,0:T(8,128)(2,1)}, bf16[640,6144]{1,0:T(8,128)(2,1)}) fusion(f32[640]{0:T(1024)S(1)} %get-tuple-element.39, f32[]{:T(128)S(6)} %convert_element_type.19, pred[]{:T(512)S(6)} %lt.49, s32[]{:T(128)S(6)} %select_n.34, s32[640]{0:T(1024)S(1)} %copy-done.1, pred[6144]{0:T(1024)(128)(4,1)S(1)} %iota_compare_fusion.1, ...), kind=kLoop, calls=%fused_computation.9 | loop fusion | flops 66846720 | bytes 15742473 | tf_op jit(solution)/shard_map/convert
  288.8 7.4 %fusion.14 = bf16[16,1,6144]{2,0,1:T(8,128)(2,1)} fusion(bf16[16,1280]{1,0:T(8,128)(2,1)S(1)} %reshape_squeeze.3, bf16[640,6144]{1,0:T(8,128)(2,1)} %get-tuple-element.38, bf16[640,6144]{1,0:T(8,128)(2,1)} %get-tuple-element.37), kind=kOutput, calls=%fused_computation.16 | convolution fusion | flops 283213824 | bytes 15966208 | tf_op jit(solution)/shard_map/dot_general | solution.py:37
  (69 shorter events, 19.8 us)
Async XLA Ops:
  0.0 2.8 copy-start
  5.0 70.2 %copy-start.1 = (s32[640]{0:T(1024)S(1)}, s32[640]{0:T(1024)}, u32[]{:S(2)}) copy-start(s32[640]{0:T(1024)} %param.6) | copy-start | bytes 7684
  66.1 221.8 %all-to-all-start = ((bf16[32,2,320]{2,1,0:T(2,128)(2,1)}), bf16[32,2,320]{2,1,0:T(2,128)(2,1)S(1)}, u32[]{:S(2)}, u32[]{:S(2)}) async-start(bf16[32,2,320]{2,1,0:T(2,128)(2,1)} %reshape.38), calls=%async_computation | async-start | bytes 98304 | tf_op jit(solution)/shard_map/all_to_all | solution.py:17
